TPU v7x, 512 devices: a whole 4x4x16 slice. The times are simulated.
512 devices in a mesh: group: 16 (over z), sub: 32 (over x, y, core).
Axes of the slice: x: 4, y: 4, z: 16, core: 2. Of those that a mesh axis runs over, the one named last changes fastest.
Arguments:
- schur_blocks: bfloat16 [16, 32, 32, 14, 4096], P('group', 'sub'), may hold values from -0.1875 to 0.1875
- block_cols: int32 [16, 32, 32, 14], P('group', 'sub'), may hold values from 0 to 31
- basis: bfloat16 [16, 32, 32, 1024], P('group', 'sub'), may hold values from -6 to 6
- owners: int32 [16, 32, 32, 1], P('group', 'sub'), may hold values from 0 to 31; in each aligned block of 32 rows (0 to 31, 32 to 63, ..., all dimensions but the last counted through in order) at most 4 rows name the same one
- targets: int32 [16, 32, 32], P('group', 'sub'), may hold values from 0 to 31
- inverses: float32 [16, 32, 32, 4096], P('group', 'sub'), may hold values from -0.75 to 0.75
- coarse_map: int32 [16, 32, 16], P('group', 'sub'), may hold values from 0 to 511
Outputs:
- corrected: float32 [16, 32, 32, 1024], P('group', 'sub')
- coarse_matrix: float32 [512, 512], P('sub')
Inputs may be any that keep to these rules, and one draw needn't show every extreme that they name: `owners`: among the 32 blocks of one subdomain at most 4 name the same owner.
All inputs are finite; a program needn't handle non-finite values.
Results may differ from a plain program's by a relative error of at most 0.0066.
Values may be sent and summed in bfloat16 or wider, within the bound.
A program may use at most 64 MiB of HBM per device.

v0:
```python
import jax
import jax.numpy as jnp
from jax import lax
from jax.sharding import PartitionSpec as P

BS = 64


def block_product(blocks, cols, vectors):
    nb = blocks.shape[0]
    kb = blocks.shape[1]
    width = vectors.shape[1] // BS
    picked = vectors[cols].reshape(nb, kb, width, BS)
    out = jnp.einsum(
        "bkij,bkcj->bci", blocks.reshape(nb, kb, BS, BS), picked, preferred_element_type=jnp.float32
    )
    return out.reshape(nb, width * BS)


def on_device(schur_blocks, block_cols, basis, owners, targets, inverses, coarse_map):
    blocks = schur_blocks[0, 0]
    cols = block_cols[0, 0]
    vectors = basis[0, 0]
    owner = owners[0, 0, :, 0]
    target = targets[0, 0]
    inverse = inverses[0, 0]
    cmap = coarse_map[0, 0]
    nsub = lax.axis_size("sub")
    nblocks = vectors.shape[0]
    width = vectors.shape[1] // BS
    capacity = max(2, 4 * nblocks // nsub)
    owned = inverse.shape[0]
    partial_value = block_product(blocks, cols, vectors).astype(jnp.bfloat16)
    owner_hot = (owner[:, None] == jnp.arange(nsub, dtype=jnp.int32)[None, :]).astype(jnp.int32)
    rank = jnp.sum(jnp.cumsum(owner_hot, axis=0) * owner_hot, axis=1) - 1
    slot = owner * capacity + rank
    select = slot[None, :] == jnp.arange(nsub * capacity, dtype=jnp.int32)[:, None]
    send = jnp.dot(
        select.astype(jnp.bfloat16), partial_value, preferred_element_type=jnp.float32
    ).astype(jnp.bfloat16)
    tags = (jnp.sum(jnp.where(select, target[None, :] + 1, 0), axis=1) - 1).reshape(-1, 1)
    arrived, arrived_tags = (
        lax.all_to_all(send, "sub", split_axis=0, concat_axis=0, tiled=True),
        lax.all_to_all(tags, "sub", split_axis=0, concat_axis=0, tiled=True),
    )
    owned_hot = (arrived_tags == jnp.arange(owned, dtype=jnp.int32)[None, :]).astype(jnp.bfloat16)
    assembled = jnp.einsum("sj,sf->jf", owned_hot, arrived, preferred_element_type=jnp.float32)
    corrected = jnp.einsum(
        "jci,jik->jck",
        assembled.reshape(owned, width, BS),
        inverse.reshape(owned, BS, BS),
        precision=lax.Precision.HIGHEST,
    ).reshape(owned, width * BS)
    back = jnp.dot(
        owned_hot, corrected.astype(jnp.bfloat16), preferred_element_type=jnp.float32
    ).astype(jnp.bfloat16)
    returned = lax.all_to_all(back, "sub", split_axis=0, concat_axis=0, tiled=True)
    from_owner = jnp.einsum(
        "sb,sf->bf", select.astype(jnp.bfloat16), returned, preferred_element_type=jnp.float32
    )
    adjusted = (vectors.astype(jnp.float32) - from_owner).astype(jnp.bfloat16)
    image = block_product(blocks, cols, adjusted)
    local_galerkin = jnp.einsum(
        "bci,bei->ce",
        adjusted.astype(jnp.float32).reshape(nblocks, width, BS),
        image.reshape(nblocks, width, BS),
        precision=lax.Precision.HIGHEST,
    )
    local_galerkin = local_galerkin * (nblocks * BS) ** (-0.5)
    coarse = width * nsub
    spread = (cmap[:, None] == jnp.arange(coarse, dtype=jnp.int32)[None, :]).astype(jnp.float32)
    right_side = jnp.dot(local_galerkin, spread, precision=lax.Precision.HIGHEST)
    own_rows = lax.psum_scatter(
        jnp.dot(spread.T, right_side, precision=lax.Precision.HIGHEST),
        "sub",
        scatter_dimension=0,
        tiled=True,
    )
    matrix = lax.psum(own_rows, "group")
    return (corrected[None, None], matrix)


def solution(mesh):
    return jax.shard_map(
        on_device,
        mesh=mesh,
        in_specs=(
            P("group", "sub", None, None, None),
            P("group", "sub", None, None),
            P("group", "sub", None, None),
            P("group", "sub", None, None),
            P("group", "sub", None),
            P("group", "sub", None, None),
            P("group", "sub", None),
        ),
        out_specs=(P("group", "sub", None, None), P("sub", None)),
        check_vma=False,
    )
```

profile of v0, /device:TPU:2, one launch (start us, length us, event | category | flops | bytes accessed | tf_op | source)
XLA Modules:
  0.0 249.9 jit_solution(4632031527185494781)
XLA Ops:
  7.2 0.7 fusion.22
  7.9 0.1 reduce_window_sum.11
  7.9 0.8 select_reduce_fusion.1
  8.8 0.7 add_add_fusion
  9.4 0.7 add_bitcast_fusion
  10.1 0.1 select_reduce_fusion
  10.2 0.7 sub.15
  10.9 9.4 %all-to-all-start = ((s32[32,4,1]{1,2,0:T(1,128)}), s32[32,4,1]{1,2,0:T(1,128)S(1)}, u32[]{:S(2)}, u32[]{:S(2)}) async-start(s32[32,4,1]{1,2,0:T(1,128)} %bitcast.2), calls=%async_computation | async-start | bytes 32768 | tf_op jit(solution)/shard_map/all_to_all | solution.py:44
  20.4 0.7 compare_select_fusion
  21.1 0.1 copy.25
  21.2 0.1 reshape.93
  21.3 3.7 %gather_fusion = bf16[448,1024]{1,0:T(8,128)(2,1)S(1)} fusion(bf16[32,1024]{1,0:T(8,128)(2,1)} %bitcast.47, s32[1024]{0:T(1024)S(1)} %pad_clamp_fusion), kind=kCustom, calls=%fused_computation | custom fusion | bytes 1836800 | tf_op jit(solution)/shard_map/gather | solution.py:13
  24.9 1.2 reshape.88
  26.1 11.1 %reshape_squeeze.7 = bf16[32,14,64,64]{3,2,0,1:T(8,128)(2,1)} reshape(bf16[1,1,32,14,4096]{4,2,3,1,0:T(8,128)(2,1)} %param.7) | data formatting | bytes 7340032 | tf_op jit(solution)/shard_map/reshape;squeeze | solution.py:15
  37.2 0.0 copy-start.1
  37.2 0.0 copy-start
  37.2 5.1 %fusion.10 = bf16[32,16,64]{2,1,0:T(8,128)(2,1)S(1)} fusion(bf16[32,14,16,64]{3,2,1,0:T(8,128)(2,1)S(1)} %reshape.88, bf16[32,14,64,64]{3,2,0,1:T(8,128)(2,1)} %reshape_squeeze.7), kind=kOutput, calls=%fused_computation.10 | convolution fusion | flops 58753024 | bytes 4653056 | tf_op jit(solution)/shard_map/bkij,bkcj->bci/dot_general | solution.py:14
  42.3 0.2 convert_element_type.34
  42.5 0.3 convolution_convert_fusion.1
  42.8 0.8 all_to_all.21
  43.6 0.0 all-to-all-done
  43.6 7.5 %all-to-all-start.1 = ((bf16[32,4,1024]{2,1,0:T(4,128)(2,1)}), bf16[32,4,1024]{2,1,0:T(4,128)(2,1)S(1)}, u32[]{:S(2)}, u32[]{:S(2)}) async-start(bf16[32,4,1024]{2,1,0:T(4,128)(2,1)} %all_to_all.21), calls=%async_computation.1 | async-start | bytes 524288 | tf_op jit(solution)/shard_map/all_to_all | solution.py:43
  51.1 0.0 reduce-scatter.2.cloned.1.call-start
  51.2 0.0 copy-done.1
  51.2 0.4 reshape_squeeze.8
  51.6 0.5 broadcast.73
  52.1 0.7 reduce.3
  52.8 0.1 eq.62
  52.9 5.9 %all-to-all-done.1 = bf16[32,4,1024]{2,1,0:T(4,128)(2,1)S(1)} async-done(((bf16[32,4,1024]{2,1,0:T(4,128)(2,1)}), bf16[32,4,1024]{2,1,0:T(4,128)(2,1)S(1)}, u32[]{:S(2)}, u32[]{:S(2)}) %all-to-all-start.1) | async-done | bytes 262176 | tf_op jit(solution)/shard_map/all_to_all | solution.py:43
  58.8 0.1 all_to_all.23
  58.9 0.2 copy.27
  59.1 0.3 fusion.23
  59.4 1.1 fusion.29
  60.6 0.1 convert_element_type.38
  60.7 0.3 convolution_convert_fusion
  61.0 0.1 all_to_all.24
  61.1 12.5 %all_to_all.30 = bf16[32,4,1024]{2,1,0:T(4,128)(2,1)S(1)} all-to-all(bf16[32,4,1024]{2,1,0:T(4,128)(2,1)S(1)} %all_to_all.24), channel_id=1, replica_groups=mesh['group'=16,'sub'=32] {'sub'}, dimensions={0} | all-to-all | bytes 524288 | tf_op jit(solution)/shard_map/all_to_all | solution.py:57
  73.6 0.1 all_to_all.26
  73.6 0.0 copy-done
  73.6 0.2 fusion.13
  73.8 0.2 reshape.89
  74.0 2.1 gather_fusion.1
  76.1 0.0 copy-start.2
  76.1 1.2 reshape.90
  77.3 5.1 %fusion.7 = f32[32,16,64]{2,1,0:T(8,128)S(1)} fusion(bf16[32,14,16,64]{3,2,1,0:T(8,128)(2,1)S(1)} %reshape.90, bf16[32,14,64,64]{3,2,0,1:T(8,128)(2,1)} %reshape_squeeze.7), kind=kOutput, calls=%fused_computation.9 | convolution fusion | flops 58720256 | bytes 4718592 | tf_op jit(solution)/shard_map/bkij,bkcj->bci/dot_general | solution.py:14
  82.4 0.3 fusion.14
  82.7 0.0 copy-done.2
  82.7 0.2 fusion.18
  82.9 1.7 fusion.17
  84.6 0.0 reduce-scatter.2.cloned.1.call-update
  84.7 0.8 broadcast_in_dim_reshape.3
  85.4 99.6 %reduce-scatter.2.cloned.1.call-done = f32[16,512]{1,0:T(8,128)} async-done(((f32[512,512]{1,0:T(8,128)}), f32[16,512]{1,0:T(8,128)}) %reduce-scatter.2.cloned.1.call-update) | async-done | bytes 32784 | tf_op jit(solution)/shard_map/reduce_scatter | solution.py:73
  185.0 58.0 %psum.7 = f32[16,512]{1,0:T(8,128)} all-reduce(f32[16,512]{1,0:T(8,128)} %reduce-scatter.2.cloned.1.call-done), channel_id=1, replica_groups=mesh['group'=16,'sub'=32] {'group'}, use_global_device_ids=true, to_apply=%region_4.5 | all-reduce | flops 8192 | bytes 65536 | tf_op jit(solution)/shard_map/psum | solution.py:79
  (2 shorter events, 0.0 us)
Async XLA Ops:
  10.9 32.7 %all-to-all-start = ((s32[32,4,1]{1,2,0:T(1,128)}), s32[32,4,1]{1,2,0:T(1,128)S(1)}, u32[]{:S(2)}, u32[]{:S(2)}) async-start(s32[32,4,1]{1,2,0:T(1,128)} %bitcast.2), calls=%async_computation | async-start | bytes 32768 | tf_op jit(solution)/shard_map/all_to_all | solution.py:44
  37.2 14.0 %copy-start.1 = (f32[1,1,32,4096]{3,2,1,0:T(8,128)S(1)}, f32[1,1,32,4096]{3,2,1,0:T(8,128)}, u32[]{:S(2)}) copy-start(f32[1,1,32,4096]{3,2,1,0:T(8,128)} %param.12) | copy-start | bytes 1572868
  37.2 36.4 %copy-start = (bf16[1,1,32,1024]{3,2,1,0:T(8,128)(2,1)S(1)}, bf16[1,1,32,1024]{3,2,1,0:T(8,128)(2,1)}, u32[]{:S(2)}) copy-start(bf16[1,1,32,1024]{3,2,1,0:T(8,128)(2,1)} %param.9) | copy-start | bytes 196612
  43.6 15.2 %all-to-all-start.1 = ((bf16[32,4,1024]{2,1,0:T(4,128)(2,1)}), bf16[32,4,1024]{2,1,0:T(4,128)(2,1)S(1)}, u32[]{:S(2)}, u32[]{:S(2)}) async-start(bf16[32,4,1024]{2,1,0:T(4,128)(2,1)} %all_to_all.21), calls=%async_computation.1 | async-start | bytes 524288 | tf_op jit(solution)/shard_map/all_to_all | solution.py:43
  51.1 133.9 %reduce-scatter.2.cloned.1.call-start = ((), (), s32[]{:S(2)}) async-start(), calls=%async_computation.4 | async-start | bytes 1081344 | tf_op jit(solution)/shard_map/reduce_scatter | solution.py:73
  76.1 6.6 %copy-start.2 = (s32[1,1,16]{2,1,0:T(1,128)S(1)}, s32[1,1,16]{2,1,0:T(1,128)}, u32[]{:S(2)}) copy-start(s32[1,1,16]{2,1,0:T(1,128)} %param.13) | copy-start | bytes 196
Sparse Core Ops, SparseCore 0:
  84.8 100.1 reduce-scatter.1
where the time goes:
time: 251 us; the launch traced here: 250 us
  waiting for transfers between devices  106 us (42%)
  blocking collectives  70.5 us (28%)
  local copies, waits for them, and re-layouts  23.6 us (9%)
  starting transfers between devices  16.9 us (7%)
  matrix products  14.7 us (6%)
  between operations  14.2 us (6%)
  other arithmetic  4.44 us (2%)
    reduce_scatter x1, waiting for transfers between devices, on_device(): lax.psum_scatter(jnp.dot(spread.T, right_side, precision=lax.Precision.HI...  99.6 us
    psum x1, blocking collectives, on_device(): matrix = lax.psum(own_rows, 'group')  58 us
    all_to_all x1, blocking collectives, on_device(): lax.all_to_all(back, 'sub', split_axis=0, concat_axis=0, tiled=True)  12.5 us
    another operation x1, local copies, waits for them, and re-layouts, block_product(): blocks.reshape(nb, kb, BS, BS)  11.1 us
    dot_general x2, matrix products, block_product(): jnp.einsum('bkij,bkcj->bci', blocks.reshape(nb, kb, BS, BS), picked, pref...  10.2 us
    all_to_all x1, starting transfers between devices, on_device(): lax.all_to_all(tags, 'sub', split_axis=0, concat_axis=0, tiled=True)  9.44 us
    all_to_all x1, starting transfers between devices, on_device(): lax.all_to_all(send, 'sub', split_axis=0, concat_axis=0, tiled=True)  7.45 us
    all_to_all x1, waiting for transfers between devices, on_device(): lax.all_to_all(send, 'sub', split_axis=0, concat_axis=0, tiled=True)  5.93 us
  transfers between devices with their start and end apart: 3, of which 2 were waited for; matrix products, arithmetic and copies ran while one was open for 10% of the time, Pallas kernels for 0%

commit v1 on v0

v1 whole, which is shorter than its diff:
```python
import functools

import jax
import jax.numpy as jnp
from jax import lax
from jax.experimental import pallas as pl
from jax.experimental.pallas import tpu as pltpu
from jax.sharding import PartitionSpec as P

MESH = pl.DeviceIdType.MESH
F32 = jnp.float32
BF16 = jnp.bfloat16
NB = 32
KB = 14
S = 32
G = 16
CAP = 4
COARSE = 512
CHUNKS = 7


def iota(shape, axis):
    return lax.broadcasted_iota(jnp.int32, shape, axis)


def hot(condition):
    return jnp.where(condition, 1.0, 0.0).astype(BF16)


def dot(a, b):
    return jnp.dot(a, b, preferred_element_type=F32)


def dot_t(a, b):
    return lax.dot_general(a, b, (((1,), (1,)), ((), ())), preferred_element_type=F32)


def lanes(v):
    return pl.ds(128 * v, 128)


def sub_peer(s, step):
    x = lax.rem(lax.div(s, 8) + lax.div(step, 8), 4)
    y = lax.rem(lax.div(s, 2) + lax.div(step, 2), 4)
    core = lax.rem(s + step, 2)
    return x * 8 + y * 2 + core


def group_peer(g, step):
    return lax.rem(g + step, G)


def spread(x):
    x3 = x.reshape(NB, 8, 128)
    r3 = pltpu.roll(x, 64, 1).reshape(NB, 8, 128)
    low = iota((NB, 8, 128), 2) < 64
    parts = [jnp.where(low, x3, 0.0), jnp.where(low, r3, 0.0), jnp.where(low, 0.0, r3), jnp.where(low, 0.0, x3)]
    return jnp.concatenate(parts, axis=1).astype(BF16)


def kernel(
    schur, cols, basis, owner, target, inverse, cmap,
    corrected, matrix,
    raw, packed, vecs, natural, rows_f32, select_t, table, send, arrive, right, pair, back, returned,
    left_g, high_g, low_g, terms, piece, pieces, final, load_sem, sem,
):
    g, s = lax.axis_index("group"), lax.axis_index("sub")

    def each(count, function):
        def body(step, carry):
            function(step)
            return carry

        lax.fori_loop(1, count, body, 0)

    def to_sub(source_of, into, k):
        def one(step):
            d = sub_peer(s, step)
            pltpu.make_async_remote_copy(
                src_ref=source_of(d), dst_ref=into.at[s], send_sem=sem.at[2 * k], recv_sem=sem.at[2 * k + 1],
                device_id={"sub": d}, device_id_type=MESH,
            ).start()

        each(S, one)

    def to_group(source_of, into, k):
        def one(step):
            d = group_peer(g, step)
            pltpu.make_async_remote_copy(
                src_ref=source_of(d), dst_ref=into.at[g], send_sem=sem.at[2 * k], recv_sem=sem.at[2 * k + 1],
                device_id={"group": d}, device_id_type=MESH,
            ).start()

        each(G, one)

    def settle(buffer, count, which):
        part = buffer.at[pl.ds(0, count)]
        pltpu.make_async_copy(part, part, sem.at[which]).wait()

    barrier = pltpu.get_barrier_semaphore()
    each(S, lambda step: pl.semaphore_signal(barrier, 1, device_id={"sub": sub_peer(s, step)}, device_id_type=MESH))
    each(G, lambda step: pl.semaphore_signal(barrier, 1, device_id={"group": group_peer(g, step)}, device_id_type=MESH))

    per = KB // CHUNKS

    def load(c):
        part = pl.ds(per * c, per)
        return pltpu.make_async_copy(schur.at[part], raw.at[part], load_sem.at[c])

    for c in range(CHUNKS):
        load(c).start()

    lane32 = iota((NB, 128), 1)
    row32 = iota((NB, 128), 0)
    eye32 = iota((NB, NB), 0) == iota((NB, NB), 1)
    own = jnp.sum(jnp.where(eye32, owner[...], 0), axis=1, keepdims=True) == lane32 // CAP
    below = hot(iota((NB, NB), 1) < iota((NB, NB), 0))
    seen = dot(below, hot(own)).astype(jnp.int32)
    taken = own & (seen == lane32 % CAP)
    target_col = jnp.sum(jnp.where(eye32, target[...].astype(F32), 0.0), axis=1, keepdims=True)
    slot_target = jnp.sum(jnp.where(taken, target_col + 1.0, 0.0), axis=0, keepdims=True)
    slot_col = jnp.sum(jnp.where(taken, lane32.astype(F32), 0.0), axis=1, keepdims=True)
    slot_row = jnp.sum(jnp.where(eye32, slot_col, 0.0), axis=0, keepdims=True)
    eye16 = iota((16, 16), 0) == iota((16, 16), 1)
    cmap_col = jnp.sum(jnp.where(eye16, cmap[...], 0), axis=1, keepdims=True)
    lane16 = iota((16, 128), 1)
    ordered = (lane16 < 16) & (iota((16, 128), 0) == 2 * (lane16 % 8) + lane16 // 8)
    map_high = jnp.sum(jnp.where(ordered, (cmap_col // 16).astype(F32), 0.0), axis=0, keepdims=True)
    map_low = jnp.sum(jnp.where(ordered, (cmap_col % 16).astype(F32), 0.0), axis=0, keepdims=True)
    table[s] = jnp.concatenate([slot_target, map_high, map_low, jnp.zeros((5, 128), F32)], axis=0)

    flat = jnp.concatenate([basis[:, lanes(u)] for u in range(8)], axis=0)
    r256, c256 = iota((256, 256), 0), iota((256, 256), 1)
    by_block = hot((c256 % NB == r256 // 8) & (c256 // NB == r256 % 8))
    nat = dot(by_block, flat)
    natural[...] = nat
    vecs[...] = spread(nat)

    regroup = hot((c256 % 16 == r256 // 16) & (c256 // 16 == r256 % 16))

    def unpack(k, half):
        at = pl.ds(pl.multiple_of(16 * half, 16), 16)
        sides = []
        for h in range(2):
            sides.append(jnp.concatenate([raw[k, at, lanes(16 * h + t)] for t in range(16)], axis=0))
        out = dot(regroup, jnp.concatenate(sides, axis=1)).astype(BF16)
        for h in range(2):
            for b in range(16):
                packed[16 * half + b, pl.ds(16 * h, 16), lanes(k)] = out[16 * b : 16 * b + 16, 128 * h : 128 * h + 128]

    for c in range(CHUNKS):
        load(c).wait()
        for k in range(per * c, per * c + per):

            def some(half, carry, k=k):
                unpack(k, half)
                return carry

            lax.fori_loop(0, 2, some, 0)

    pl.semaphore_wait(barrier, S - 1 + G - 1)
    to_sub(lambda d: table.at[s], table, 0)

    def product(b):
        vectors = jnp.concatenate([vecs[cols[k, b]] for k in range(KB)], axis=1)
        block = packed[b]
        out = dot_t(vectors, jnp.concatenate([block] * 4, axis=0))
        return [out[8 * v : 8 * v + 8] for v in range(4)]

    group8 = iota((8, 128), 1) // 32

    def first(b, carry):
        r = product(b)
        value = jnp.where(group8 == 0, r[0], jnp.where(group8 == 1, r[1], jnp.where(group8 == 2, r[2], r[3])))
        rows_f32[pl.ds(pl.multiple_of(8 * b, 8), 8), :] = value
        return carry

    lax.fori_loop(0, NB, first, 0, unroll=4)

    widen = hot(iota((NB, 256), 1) // 8 == iota((NB, 256), 0))
    slot_lane = dot(jnp.broadcast_to(slot_row, (8, NB)).astype(BF16), widen)[0:1].astype(jnp.int32)
    code = slot_lane // CAP * 32 + iota((1, 256), 1) % 8 * CAP + slot_lane % CAP
    select = hot(iota((1024, 256), 0) == code)
    send[...] = dot(select, rows_f32[...].astype(BF16)).astype(BF16).reshape(S, 32, 128)
    to_sub(lambda d: send.at[d], arrive, 1)
    arrive[s] = send[s]

    tall = hot(iota((256, NB), 0) // 8 == iota((256, NB), 1))
    slot_tall = dot(tall, jnp.broadcast_to(slot_col, (NB, 128)).astype(BF16)).astype(jnp.int32)
    code_tall = slot_tall // CAP * 32 + iota((256, 128), 0) % 8 * CAP + slot_tall % CAP
    for v in range(8):
        select_t[:, lanes(v)] = hot(iota((256, 128), 1) + 128 * v == code_tall)

    for jg in range(4):
        tiles = jnp.stack([inverse[pl.ds(8 * jg, 8), lanes(t)] for t in range(32)], axis=0)
        block = jnp.swapaxes(tiles, 0, 1)
        turned = pltpu.roll(block.reshape(256, 128), 64, 1).reshape(8, 32, 128)
        low = iota((8, 32, 128), 2) < 64
        parts = [jnp.where(low, block, 0.0), jnp.where(low, 0.0, turned), jnp.where(low, turned, 0.0), jnp.where(low, 0.0, block)]
        right[pl.ds(8 * jg, 8)] = jnp.concatenate(parts, axis=1).astype(BF16)

    settle(table, S - 1, 1)
    mine = jnp.where(lane32 // CAP == s, table[:, 0, :], 0.0).astype(BF16)
    by_slot = hot(iota((128, 1024), 0) % CAP == iota((128, 1024), 1) % CAP)
    spread_slot = dot(mine, by_slot)
    named = jnp.sum(jnp.where(iota((NB, 1024), 0) == iota((NB, 1024), 1) // 32, spread_slot, 0.0), axis=0, keepdims=True)
    code_in = (named.astype(jnp.int32) - 1) * 8 + iota((1, 1024), 1) // CAP % 8
    gather = hot(iota((256, 1024), 0) == code_in)
    by_source = hot(iota((1024, NB), 0) // 32 == iota((1024, NB), 1))
    tall_slot = dot(by_source, mine)
    kept = jnp.where(iota((1024, 128), 0) % CAP == iota((1024, 128), 1) % CAP, tall_slot, 0.0).astype(BF16)
    named_t = dot(kept, jnp.full((128, 256), 1.0, BF16)).astype(jnp.int32)
    gather_t = hot(iota((1024, 256), 1) == (named_t - 1) * 8 + iota((1024, 256), 0) // CAP % 8)

    settle(arrive, S - 1, 3)
    assembled = dot(gather, arrive[...].reshape(1024, 128))
    high = assembled.astype(BF16).astype(F32)
    pair[...] = jnp.concatenate(
        [high.reshape(NB, 8, 128), (assembled - high).reshape(NB, 8, 128)], axis=1
    ).astype(BF16)

    def correct(j, carry):
        out = dot(pair[j], right[j])
        rows_f32[pl.ds(pl.multiple_of(8 * j, 8), 8), :] = out[0:8] + out[8:16]
        return carry

    lax.fori_loop(0, NB, correct, 0, unroll=8)
    back[...] = dot(gather_t, rows_f32[...].astype(BF16)).astype(BF16).reshape(S, 32, 128)
    to_sub(lambda d: back.at[d], returned, 2)
    returned[s] = back[s]
    for u in range(8):
        corrected[:, lanes(u)] = rows_f32[pl.ds(u, NB, stride=8), :]

    erep_l = iota((128, 256), 1)
    copies = hot(iota((128, 256), 0) == erep_l // 128 * 16 + erep_l % 16)
    maps_h = table[:, 1, :].astype(BF16)
    maps_l = table[:, 2, :].astype(BF16)
    ll = iota((128, 1024), 1)
    pick = hot(iota((128, 1024), 0) == ll // 64 % 2 * 8 + ll % 8)
    source = ll[0:NB] // 256 * 8 + ll[0:NB] // 8 % 8
    is_source = iota((NB, 1024), 0) == source
    lane_h = jnp.sum(jnp.where(is_source, dot(maps_h, pick), 0.0), axis=0, keepdims=True).astype(jnp.int32)
    lane_l = jnp.sum(jnp.where(is_source, dot(maps_l, pick), 0.0), axis=0, keepdims=True).astype(jnp.int32)
    rows_mine = hot((iota((16, 1024), 0) == lane_l) & (lane_h == s))
    tall_s = hot(iota((512, NB), 0) // 16 == iota((512, NB), 1))
    own_lane = iota((512, 128), 0) % 16 == iota((512, 128), 1)
    col_h = jnp.where(own_lane, dot(tall_s, maps_h), 0.0).astype(BF16)
    col_l = jnp.where(own_lane, dot(tall_s, maps_l), 0.0).astype(BF16)
    ones = jnp.full((128, COARSE), 1.0, BF16)
    place = (dot(col_h, ones) * 16.0 + dot(col_l, ones)).astype(jnp.int32)
    spread_cols = hot(place == iota((512, COARSE), 1))

    settle(returned, S - 1, 5)
    from_owner = dot(select_t[...], returned[...].reshape(1024, 128))
    adjusted = (natural[...] - from_owner).astype(BF16)
    vecs[...] = spread(adjusted.astype(F32))
    q_row, q_col = iota((128, 128), 0), iota((128, 128), 1)
    reorder = hot((q_row // 64 == q_col // 32 % 2) & (q_row % 2 == q_col // 64) & (q_row % 64 // 2 == q_col % 32))
    message = dot(adjusted, reorder).reshape(NB, 8, 128)
    for b in range(NB):
        left_g[:, lanes(b)] = jnp.concatenate([message[b], jnp.zeros((8, 128), F32)], axis=0).astype(BF16)

    def second(b, carry):
        r = product(b)
        at_low = group8 < 2
        p_low = group8 % 2 == 0
        one, two = jnp.where(at_low, r[0], r[2]), jnp.where(at_low, r[1], r[3])
        rows = jnp.concatenate(
            [jnp.where(p_low, one, 0.0), jnp.where(p_low, two, 0.0), jnp.where(p_low, 0.0, one), jnp.where(p_low, 0.0, two)],
            axis=0,
        )
        top = rows.astype(BF16)
        at = pl.ds(pl.multiple_of(128 * b, 128), 128)
        high_g[:, at] = top
        low_g[:, at] = (rows - top.astype(F32)).astype(BF16)
        return carry

    lax.fori_loop(0, NB, second, 0, unroll=4)
    galerkin = (dot_t(left_g[...], high_g[...]) + dot_t(left_g[...], low_g[...])) * (NB * 64) ** -0.5
    terms[s] = jnp.concatenate([galerkin[0:8], jnp.zeros((8, 96), F32)], axis=1)
    to_sub(lambda d: terms.at[s], terms, 3)

    settle(terms, S - 1, 7)
    every = terms[...].reshape(256, 128)
    top = every.astype(BF16)
    both = jnp.concatenate([top, (every - top.astype(F32)).astype(BF16)], axis=0)
    wide = dot(both, copies)
    wide_row, wide_lane = iota((512, 256), 0), iota((512, 256), 1)
    wide = jnp.where(wide_row // 8 % 8 == wide_lane // 16 % 8, wide, 0.0).astype(BF16)
    parts = []
    for v in range(4):
        pieces_v = [wide[256 * h + 64 * v : 256 * h + 64 * v + 64, 128 * p : 128 * p + 128] for h in range(2) for p in range(2)]
        parts.append(dot(rows_mine[:, 256 * v : 256 * v + 256], jnp.concatenate(pieces_v, axis=0)))
    part = jnp.concatenate(parts, axis=1)
    p1 = part.astype(BF16).astype(F32)
    p2 = (part - p1).astype(BF16).astype(F32)
    p3 = part - p1 - p2
    out = dot(jnp.concatenate([p1, p2, p3], axis=0).astype(BF16), spread_cols)
    out = out[0:16] + out[16:32] + out[32:48]
    for v in range(G):
        piece[v] = out[4 * (v // 4) : 4 * (v // 4) + 4, 128 * (v % 4) : 128 * (v % 4) + 128]
    to_group(lambda d: piece.at[d], pieces, 4)
    pieces[g] = piece[g]
    settle(pieces, G - 1, 9)
    total = pieces[0]
    for v in range(1, G):
        total = total + pieces[v]
    final[g] = total
    to_group(lambda d: final.at[g], final, 5)
    settle(final, G - 1, 11)
    for v in range(G):
        matrix[pl.ds(4 * (v // 4), 4), lanes(v % 4)] = final[v]

    settle(table, S - 1, 0)
    settle(send, S - 1, 2)
    settle(back, S - 1, 4)
    settle(terms, S - 1, 6)
    settle(piece, G - 1, 8)
    settle(final, G - 1, 10)


def on_device(schur_blocks, block_cols, basis, owners, targets, inverses, coarse_map):
    vmem = pl.BlockSpec(memory_space=pltpu.VMEM)
    corrected, matrix = pl.pallas_call(
        kernel,
        out_shape=(jax.ShapeDtypeStruct((NB, 1024), F32), jax.ShapeDtypeStruct((16, COARSE), F32)),
        in_specs=[pl.BlockSpec(memory_space=pltpu.HBM), pl.BlockSpec(memory_space=pltpu.SMEM)] + [vmem] * 5,
        out_specs=(vmem, vmem),
        scratch_shapes=[
            pltpu.VMEM((KB, NB, 4096), BF16),
            pltpu.VMEM((NB, 32, 128 * KB), BF16),
            pltpu.VMEM((NB, 32, 128), BF16),
            pltpu.VMEM((256, 128), F32),
            pltpu.VMEM((256, 128), F32),
            pltpu.VMEM((256, 1024), BF16),
            pltpu.VMEM((S, 8, 128), F32),
            pltpu.VMEM((S, 32, 128), BF16),
            pltpu.VMEM((S, 32, 128), BF16),
            pltpu.VMEM((NB, 128, 128), BF16),
            pltpu.VMEM((NB, 16, 128), BF16),
            pltpu.VMEM((S, 32, 128), BF16),
            pltpu.VMEM((S, 32, 128), BF16),
            pltpu.VMEM((16, 128 * NB), BF16),
            pltpu.VMEM((32, 128 * NB), BF16),
            pltpu.VMEM((32, 128 * NB), BF16),
            pltpu.VMEM((S, 8, 128), F32),
            pltpu.VMEM((G, 4, 128), F32),
            pltpu.VMEM((G, 4, 128), F32),
            pltpu.VMEM((G, 4, 128), F32),
            pltpu.SemaphoreType.DMA((CHUNKS,)),
            pltpu.SemaphoreType.DMA((12,)),
        ],
        compiler_params=pltpu.CompilerParams(
            collective_id=0, has_side_effects=True, vmem_limit_bytes=48 * 1024 * 1024
        ),
        name="setup_pass",
    )(
        jnp.swapaxes(schur_blocks[0, 0], 0, 1),
        block_cols[0, 0].T,
        basis[0, 0],
        owners[0, :, :, 0],
        targets[0],
        inverses[0, 0],
        coarse_map[0],
    )
    return corrected[None, None], matrix


def solution(mesh):
    return jax.shard_map(
        on_device,
        mesh=mesh,
        in_specs=(
            P("group", "sub", None, None, None),
            P("group", "sub", None, None),
            P("group", "sub", None, None),
            P("group", "sub", None, None),
            P("group", "sub", None),
            P("group", "sub", None, None),
            P("group", "sub", None),
        ),
        out_specs=(P("group", "sub", None, None), P("sub", None)),
        check_vma=False,
    )
```

time: 251 us -> 74.1 us (0.30)
  the two profiles are of different devices: /device:TPU:2 before, /device:TPU:1 now
where the time goes in v1:
time: 74.1 us; the launch traced here: 73.8 us
  Pallas kernels  65.3 us (88%)
  local copies, waits for them, and re-layouts  7.85 us (11%)
    pallas_call x1, Pallas kernels, on_device(): pl.pallas_call(kernel, out_shape=(jax.ShapeDtypeStruct((NB, 1024), F32),...  65.3 us
    unnamed x15, local copies, waits for them, and re-layouts  7.85 us

profile of v1, /device:TPU:1, one launch (start us, length us, event | category | flops | bytes accessed | tf_op | source)
XLA Modules:
  0.0 73.8 jit_solution(4417842049228415850)
XLA Ops:
  0.6 0.7 copy.11
  1.3 0.0 copy-start
  1.3 2.0 %copy-done = bf16[1,1,32,14,4096]{4,2,3,1,0:T(8,128)(2,1)S(1)} copy-done((bf16[1,1,32,14,4096]{4,2,3,1,0:T(8,128)(2,1)S(1)}, bf16[1,1,32,14,4096]{4,2,3,1,0:T(8,128)(2,1)}, u32[]{:S(2)}) %copy-start) | copy-done | bytes 3670040
  3.4 0.0 copy-start.1
  3.4 1.0 %copy-done.1 = f32[1,1,32,4096]{3,2,1,0:T(8,128)S(1)} copy-done((f32[1,1,32,4096]{3,2,1,0:T(8,128)S(1)}, f32[1,1,32,4096]{3,2,1,0:T(8,128)}, u32[]{:S(2)}) %copy-start.1) | copy-done | bytes 524312
  4.4 0.0 copy-start.2
  4.4 0.8 %copy-done.2 = bf16[1,1,32,1024]{3,2,1,0:T(8,128)(2,1)S(1)} copy-done((bf16[1,1,32,1024]{3,2,1,0:T(8,128)(2,1)S(1)}, bf16[1,1,32,1024]{3,2,1,0:T(8,128)(2,1)}, u32[]{:S(2)}) %copy-start.2) | copy-done | bytes 65560
  5.2 0.0 copy-start.3
  5.2 0.7 copy-done.3
  5.9 0.0 copy-start.4
  5.9 0.7 copy-done.4
  6.6 0.0 copy-start.5
  6.6 0.7 copy-done.5
  7.2 65.3 %setup_pass.1 = (f32[32,1024]{1,0:T(8,128)S(1)}, f32[16,512]{1,0:T(8,128)S(1)}) custom-call(bf16[14,32,4096]{2,1,0:T(8,128)(2,1)S(1)} %bitcast.14, s32[14,32]{1,0:T(8,128)S(1)} %bitcast.18, bf16[32,1024]{1,0:T(8,128)(2,1)S(1)} %bitcast.17, s32[1,32]{1,0:T(1,128)S(1)} %bitcast.19, s32[1,32]{1,0:T(1,128)S(1)} %bitcast.20, f32[32,4096]{1,0:T(8,128)S(1)} %bitcast.15, ...), custom_call_target="tpu_custom_call" | custom-call | tf_op jit(solution)/shard_map/setup_pass/pallas_call | solution.py:324
  72.5 0.7 copy.14
  73.2 0.6 copy.15
Async XLA Ops:
  1.3 2.0 %copy-start = (bf16[1,1,32,14,4096]{4,2,3,1,0:T(8,128)(2,1)S(1)}, bf16[1,1,32,14,4096]{4,2,3,1,0:T(8,128)(2,1)}, u32[]{:S(2)}) copy-start(bf16[1,1,32,14,4096]{4,2,3,1,0:T(8,128)(2,1)} %param.7) | copy-start | bytes 11010052
  3.4 1.0 %copy-start.1 = (f32[1,1,32,4096]{3,2,1,0:T(8,128)S(1)}, f32[1,1,32,4096]{3,2,1,0:T(8,128)}, u32[]{:S(2)}) copy-start(f32[1,1,32,4096]{3,2,1,0:T(8,128)} %param.12) | copy-start | bytes 1572868
  4.4 0.8 %copy-start.2 = (bf16[1,1,32,1024]{3,2,1,0:T(8,128)(2,1)S(1)}, bf16[1,1,32,1024]{3,2,1,0:T(8,128)(2,1)}, u32[]{:S(2)}) copy-start(bf16[1,1,32,1024]{3,2,1,0:T(8,128)(2,1)} %param.9) | copy-start | bytes 196612
  5.2 0.7 copy-start.3
  5.9 0.7 copy-start.4
  6.6 0.7 copy-start.5

commit v2 on v1

--- a/solution.py
+++ b/solution.py
@@ -50,6 +50,14 @@
     return lax.rem(g + step, G)
 
 
+def ring(distance, length):
+    return min(distance, length - distance)
+
+
+SUB_STEPS = sorted(range(1, S), key=lambda v: -(ring(v // 8, 4) + ring(v // 2 % 4, 4) + 0.5 * (v % 2)))
+GROUP_STEPS = sorted(range(1, G), key=lambda v: -ring(v, G))
+
+
 def spread(x):
     x3 = x.reshape(NB, 8, 128)
     r3 = pltpu.roll(x, 64, 1).reshape(NB, 8, 128)
@@ -59,9 +67,9 @@
 
 
 def kernel(
-    schur, cols, basis, owner, target, inverse, cmap,
+    schur, cols_hbm, basis_hbm, owner_hbm, target_hbm, inverse_hbm, cmap_hbm,
     corrected, matrix,
-    raw, packed, vecs, natural, rows_f32, select_t, table, send, arrive, right, pair, back, returned,
+    cols, basis, owner, target, inverse, cmap, raw, packed, vecs, natural, rows_f32, select_t, table, send, arrive, right, pair, back, returned,
     left_g, high_g, low_g, terms, piece, pieces, final, load_sem, sem,
 ):
     g, s = lax.axis_index("group"), lax.axis_index("sub")
@@ -81,7 +89,8 @@
                 device_id={"sub": d}, device_id_type=MESH,
             ).start()
 
-        each(S, one)
+        for step in SUB_STEPS:
+            one(step)
 
     def to_group(source_of, into, k):
         def one(step):
@@ -91,7 +100,8 @@
                 device_id={"group": d}, device_id_type=MESH,
             ).start()
 
-        each(G, one)
+        for step in GROUP_STEPS:
+            one(step)
 
     def settle(buffer, count, which):
         part = buffer.at[pl.ds(0, count)]
@@ -107,8 +117,16 @@
         part = pl.ds(per * c, per)
         return pltpu.make_async_copy(schur.at[part], raw.at[part], load_sem.at[c])
 
+    small = [(owner_hbm, owner), (target_hbm, target), (cmap_hbm, cmap), (basis_hbm, basis), (cols_hbm, cols)]
+    small = [pltpu.make_async_copy(a, b, load_sem.at[CHUNKS + v]) for v, (a, b) in enumerate(small)]
+    for copy in small:
+        copy.start()
     for c in range(CHUNKS):
         load(c).start()
+    load_inverse = pltpu.make_async_copy(inverse_hbm, inverse, load_sem.at[CHUNKS + 5])
+    load_inverse.start()
+    for copy in small:
+        copy.wait()
 
     lane32 = iota((NB, 128), 1)
     row32 = iota((NB, 128), 0)
@@ -139,7 +157,7 @@
     regroup = hot((c256 % 16 == r256 // 16) & (c256 // 16 == r256 % 16))
 
     def unpack(k, half):
-        at = pl.ds(pl.multiple_of(16 * half, 16), 16)
+        at = pl.ds(16 * half, 16)
         sides = []
         for h in range(2):
             sides.append(jnp.concatenate([raw[k, at, lanes(16 * h + t)] for t in range(16)], axis=0))
@@ -151,20 +169,15 @@
     for c in range(CHUNKS):
         load(c).wait()
         for k in range(per * c, per * c + per):
-
-            def some(half, carry, k=k):
+            for half in range(2):
                 unpack(k, half)
-                return carry
-
-            lax.fori_loop(0, 2, some, 0)
 
     pl.semaphore_wait(barrier, S - 1 + G - 1)
     to_sub(lambda d: table.at[s], table, 0)
 
     def product(b):
-        vectors = jnp.concatenate([vecs[cols[k, b]] for k in range(KB)], axis=1)
-        block = packed[b]
-        out = dot_t(vectors, jnp.concatenate([block] * 4, axis=0))
+        vectors = jnp.concatenate([vecs[cols[k, 0, b]] for k in range(KB)], axis=1)
+        out = jnp.concatenate([dot_t(vectors, packed[b])] * 4, axis=1)
         return [out[8 * v : 8 * v + 8] for v in range(4)]
 
     group8 = iota((8, 128), 1) // 32
@@ -175,7 +188,7 @@
         rows_f32[pl.ds(pl.multiple_of(8 * b, 8), 8), :] = value
         return carry
 
-    lax.fori_loop(0, NB, first, 0, unroll=4)
+    lax.fori_loop(0, NB, first, 0, unroll=8)
 
     widen = hot(iota((NB, 256), 1) // 8 == iota((NB, 256), 0))
     slot_lane = dot(jnp.broadcast_to(slot_row, (8, NB)).astype(BF16), widen)[0:1].astype(jnp.int32)
@@ -191,13 +204,17 @@
     for v in range(8):
         select_t[:, lanes(v)] = hot(iota((256, 128), 1) + 128 * v == code_tall)
 
+    load_inverse.wait()
     for jg in range(4):
         tiles = jnp.stack([inverse[pl.ds(8 * jg, 8), lanes(t)] for t in range(32)], axis=0)
         block = jnp.swapaxes(tiles, 0, 1)
         turned = pltpu.roll(block.reshape(256, 128), 64, 1).reshape(8, 32, 128)
         low = iota((8, 32, 128), 2) < 64
         parts = [jnp.where(low, block, 0.0), jnp.where(low, 0.0, turned), jnp.where(low, turned, 0.0), jnp.where(low, 0.0, block)]
-        right[pl.ds(8 * jg, 8)] = jnp.concatenate(parts, axis=1).astype(BF16)
+        full = jnp.concatenate(parts, axis=1)
+        top = full.astype(BF16)
+        right[pl.ds(8 * jg, 8), pl.ds(0, 128)] = top
+        right[pl.ds(8 * jg, 8), pl.ds(128, 128)] = (full - top.astype(F32)).astype(BF16)
 
     settle(table, S - 1, 1)
     mine = jnp.where(lane32 // CAP == s, table[:, 0, :], 0.0).astype(BF16)
@@ -220,7 +237,7 @@
     ).astype(BF16)
 
     def correct(j, carry):
-        out = dot(pair[j], right[j])
+        out = dot(jnp.concatenate([pair[j], pair[j]], axis=1), right[j])
         rows_f32[pl.ds(pl.multiple_of(8 * j, 8), 8), :] = out[0:8] + out[8:16]
         return carry
 
@@ -275,7 +292,7 @@
         low_g[:, at] = (rows - top.astype(F32)).astype(BF16)
         return carry
 
-    lax.fori_loop(0, NB, second, 0, unroll=4)
+    lax.fori_loop(0, NB, second, 0, unroll=8)
     galerkin = (dot_t(left_g[...], high_g[...]) + dot_t(left_g[...], low_g[...])) * (NB * 64) ** -0.5
     terms[s] = jnp.concatenate([galerkin[0:8], jnp.zeros((8, 96), F32)], axis=1)
     to_sub(lambda d: terms.at[s], terms, 3)
@@ -324,9 +341,15 @@
     corrected, matrix = pl.pallas_call(
         kernel,
         out_shape=(jax.ShapeDtypeStruct((NB, 1024), F32), jax.ShapeDtypeStruct((16, COARSE), F32)),
-        in_specs=[pl.BlockSpec(memory_space=pltpu.HBM), pl.BlockSpec(memory_space=pltpu.SMEM)] + [vmem] * 5,
+        in_specs=[pl.BlockSpec(memory_space=pltpu.HBM)] * 7,
         out_specs=(vmem, vmem),
         scratch_shapes=[
+            pltpu.SMEM((KB, 1, NB), jnp.int32),
+            pltpu.VMEM((NB, 1024), BF16),
+            pltpu.VMEM((1, NB), jnp.int32),
+            pltpu.VMEM((1, NB), jnp.int32),
+            pltpu.VMEM((NB, 4096), F32),
+            pltpu.VMEM((1, 16), jnp.int32),
             pltpu.VMEM((KB, NB, 4096), BF16),
             pltpu.VMEM((NB, 32, 128 * KB), BF16),
             pltpu.VMEM((NB, 32, 128), BF16),
@@ -336,7 +359,7 @@
             pltpu.VMEM((S, 8, 128), F32),
             pltpu.VMEM((S, 32, 128), BF16),
             pltpu.VMEM((S, 32, 128), BF16),
-            pltpu.VMEM((NB, 128, 128), BF16),
+            pltpu.VMEM((NB, 256, 128), BF16),
             pltpu.VMEM((NB, 16, 128), BF16),
             pltpu.VMEM((S, 32, 128), BF16),
             pltpu.VMEM((S, 32, 128), BF16),
@@ -347,16 +370,16 @@
             pltpu.VMEM((G, 4, 128), F32),
             pltpu.VMEM((G, 4, 128), F32),
             pltpu.VMEM((G, 4, 128), F32),
-            pltpu.SemaphoreType.DMA((CHUNKS,)),
+            pltpu.SemaphoreType.DMA((CHUNKS + 6,)),
             pltpu.SemaphoreType.DMA((12,)),
         ],
         compiler_params=pltpu.CompilerParams(
-            collective_id=0, has_side_effects=True, vmem_limit_bytes=48 * 1024 * 1024
+            collective_id=0, has_side_effects=True, vmem_limit_bytes=62 * 1024 * 1024
         ),
         name="setup_pass",
     )(
         jnp.swapaxes(schur_blocks[0, 0], 0, 1),
-        block_cols[0, 0].T,
+        jnp.transpose(block_cols, (0, 3, 1, 2))[0],
         basis[0, 0],
         owners[0, :, :, 0],
         targets[0],

time: 74.1 us -> 59 us (0.80)
  Pallas kernels: 65.3 us -> 55.1 us
  local copies, waits for them, and re-layouts: 7.85 us -> 2.94 us
    pallas_call x1, Pallas kernels: 65.3 us -> 55.1 us  [on_device(): pl.pallas_call(kernel, out_shape=(jax.ShapeDtypeStruct((NB, 1024), F32),...]
    unnamed x15 -> x2, local copies, waits for them, and re-layouts: 7.85 us -> 2.94 us
where the time goes in v2:
time: 59 us; the launch traced here: 58.7 us
  Pallas kernels  55.1 us (93%)
  local copies, waits for them, and re-layouts  2.94 us (5%)
  between operations  0.64 us (1%)
    pallas_call x1, Pallas kernels, on_device(): pl.pallas_call(kernel, out_shape=(jax.ShapeDtypeStruct((NB, 1024), F32),...  55.1 us
    unnamed x2, local copies, waits for them, and re-layouts  2.94 us

profile of v2, /device:TPU:1, one launch (start us, length us, event | category | flops | bytes accessed | tf_op | source)
XLA Modules:
  0.0 58.7 jit_solution(2245961493439120508)
XLA Ops:
  0.6 55.1 %setup_pass.1 = (f32[32,1024]{1,0:T(8,128)}, f32[16,512]{1,0:T(8,128)}) custom-call(bf16[14,32,4096]{2,1,0:T(8,128)(2,1)} %bitcast.12, s32[14,1,32]{2,1,0:T(1,128)} %bitcast.16, bf16[32,1024]{1,0:T(8,128)(2,1)} %bitcast.15, s32[1,32]{1,0:T(1,128)} %bitcast.17, s32[1,32]{1,0:T(1,128)} %bitcast.18, f32[32,4096]{1,0:T(8,128)} %bitcast.13, s32[1,16]{1,0:T(1,128)} %bitcast.19), custom_call_target="tpu_custom_call" | custom-call | tf_op jit(solution)/shard_map/setup_pass/pallas_call | solution.py:341
  55.8 1.6 %copy.11 = f32[1,1,32,1024]{3,2,1,0:T(8,128)} copy(f32[1,1,32,1024]{3,2,1,0:T(8,128)} %bitcast.14) | data formatting | bytes 262144
  57.4 1.4 %copy.12 = f32[16,512]{1,0:T(8,128)} copy(f32[16,512]{1,0:T(8,128)} %get-tuple-element.9) | data formatting | bytes 65536

commit v3 on v2

--- a/solution.py
+++ b/solution.py
@@ -70,7 +70,7 @@
     schur, cols_hbm, basis_hbm, owner_hbm, target_hbm, inverse_hbm, cmap_hbm,
     corrected, matrix,
     cols, basis, owner, target, inverse, cmap, raw, packed, vecs, natural, rows_f32, select_t, table, send, arrive, right, pair, back, returned,
-    left_g, high_g, low_g, terms, piece, pieces, final, load_sem, sem,
+    left_g, high_g, low_g, maps_z, maps_s, terms_z, terms_s, spread_t, load_sem, sem,
 ):
     g, s = lax.axis_index("group"), lax.axis_index("sub")
 
@@ -81,11 +81,11 @@
 
         lax.fori_loop(1, count, body, 0)
 
-    def to_sub(source_of, into, k):
+    def to_sub(source_of, into, k, landing=lambda step: 0):
         def one(step):
             d = sub_peer(s, step)
             pltpu.make_async_remote_copy(
-                src_ref=source_of(d), dst_ref=into.at[s], send_sem=sem.at[2 * k], recv_sem=sem.at[2 * k + 1],
+                src_ref=source_of(d), dst_ref=into.at[s], send_sem=sem.at[2 * k], recv_sem=sem.at[2 * k + 1 + landing(step)],
                 device_id={"sub": d}, device_id_type=MESH,
             ).start()
 
@@ -106,10 +106,6 @@
     def settle(buffer, count, which):
         part = buffer.at[pl.ds(0, count)]
         pltpu.make_async_copy(part, part, sem.at[which]).wait()
-
-    barrier = pltpu.get_barrier_semaphore()
-    each(S, lambda step: pl.semaphore_signal(barrier, 1, device_id={"sub": sub_peer(s, step)}, device_id_type=MESH))
-    each(G, lambda step: pl.semaphore_signal(barrier, 1, device_id={"group": group_peer(g, step)}, device_id_type=MESH))
 
     per = KB // CHUNKS
 
@@ -125,6 +121,10 @@
         load(c).start()
     load_inverse = pltpu.make_async_copy(inverse_hbm, inverse, load_sem.at[CHUNKS + 5])
     load_inverse.start()
+
+    barrier = pltpu.get_barrier_semaphore()
+    each(S, lambda step: pl.semaphore_signal(barrier, 1, device_id={"sub": sub_peer(s, step)}, device_id_type=MESH))
+    each(G, lambda step: pl.semaphore_signal(barrier, 1, device_id={"group": group_peer(g, step)}, device_id_type=MESH))
     for copy in small:
         copy.wait()
 
@@ -139,13 +139,11 @@
     slot_target = jnp.sum(jnp.where(taken, target_col + 1.0, 0.0), axis=0, keepdims=True)
     slot_col = jnp.sum(jnp.where(taken, lane32.astype(F32), 0.0), axis=1, keepdims=True)
     slot_row = jnp.sum(jnp.where(eye32, slot_col, 0.0), axis=0, keepdims=True)
-    eye16 = iota((16, 16), 0) == iota((16, 16), 1)
-    cmap_col = jnp.sum(jnp.where(eye16, cmap[...], 0), axis=1, keepdims=True)
-    lane16 = iota((16, 128), 1)
-    ordered = (lane16 < 16) & (iota((16, 128), 0) == 2 * (lane16 % 8) + lane16 // 8)
-    map_high = jnp.sum(jnp.where(ordered, (cmap_col // 16).astype(F32), 0.0), axis=0, keepdims=True)
-    map_low = jnp.sum(jnp.where(ordered, (cmap_col % 16).astype(F32), 0.0), axis=0, keepdims=True)
-    table[s] = jnp.concatenate([slot_target, map_high, map_low, jnp.zeros((5, 128), F32)], axis=0)
+    table[s] = jnp.concatenate([slot_target, jnp.zeros((7, 128), F32)], axis=0)
+    row16, lane16 = iota((16, 16), 0), iota((16, 16), 1)
+    cmap_col = jnp.sum(jnp.where(lane16 == 2 * (row16 % 8) + row16 // 8, cmap[...], 0), axis=1, keepdims=True)
+    place16 = iota((16, 128), 1) // 16 == lax.rem(g, 8)
+    maps_z[g] = jnp.where(place16, (cmap_col - COARSE // 2).astype(F32), 0.0).astype(BF16)
 
     flat = jnp.concatenate([basis[:, lanes(u)] for u in range(8)], axis=0)
     r256, c256 = iota((256, 256), 0), iota((256, 256), 1)
@@ -174,6 +172,7 @@
 
     pl.semaphore_wait(barrier, S - 1 + G - 1)
     to_sub(lambda d: table.at[s], table, 0)
+    to_group(lambda d: maps_z.at[g], maps_z, 3)
 
     def product(b):
         vectors = jnp.concatenate([vecs[cols[k, 0, b]] for k in range(KB)], axis=1)
@@ -248,24 +247,16 @@
     for u in range(8):
         corrected[:, lanes(u)] = rows_f32[pl.ds(u, NB, stride=8), :]
 
-    erep_l = iota((128, 256), 1)
-    copies = hot(iota((128, 256), 0) == erep_l // 128 * 16 + erep_l % 16)
-    maps_h = table[:, 1, :].astype(BF16)
-    maps_l = table[:, 2, :].astype(BF16)
-    ll = iota((128, 1024), 1)
-    pick = hot(iota((128, 1024), 0) == ll // 64 % 2 * 8 + ll % 8)
-    source = ll[0:NB] // 256 * 8 + ll[0:NB] // 8 % 8
-    is_source = iota((NB, 1024), 0) == source
-    lane_h = jnp.sum(jnp.where(is_source, dot(maps_h, pick), 0.0), axis=0, keepdims=True).astype(jnp.int32)
-    lane_l = jnp.sum(jnp.where(is_source, dot(maps_l, pick), 0.0), axis=0, keepdims=True).astype(jnp.int32)
-    rows_mine = hot((iota((16, 1024), 0) == lane_l) & (lane_h == s))
-    tall_s = hot(iota((512, NB), 0) // 16 == iota((512, NB), 1))
-    own_lane = iota((512, 128), 0) % 16 == iota((512, 128), 1)
-    col_h = jnp.where(own_lane, dot(tall_s, maps_h), 0.0).astype(BF16)
-    col_l = jnp.where(own_lane, dot(tall_s, maps_l), 0.0).astype(BF16)
-    ones = jnp.full((128, COARSE), 1.0, BF16)
-    place = (dot(col_h, ones) * 16.0 + dot(col_l, ones)).astype(jnp.int32)
-    spread_cols = hot(place == iota((512, COARSE), 1))
+    def merge(parts, into):
+        for h in range(2):
+            total = parts[8 * h].astype(F32)
+            for v in range(1, 8):
+                total = total + parts[8 * h + v].astype(F32)
+            into[s, :, lanes(h)] = total.astype(BF16)
+
+    settle(maps_z, G - 1, 7)
+    merge(maps_z, maps_s)
+    to_sub(lambda d: maps_s.at[s], maps_s, 4)
 
     settle(returned, S - 1, 5)
     from_owner = dot(select_t[...], returned[...].reshape(1024, 128))
@@ -273,19 +264,17 @@
     vecs[...] = spread(adjusted.astype(F32))
     q_row, q_col = iota((128, 128), 0), iota((128, 128), 1)
     reorder = hot((q_row // 64 == q_col // 32 % 2) & (q_row % 2 == q_col // 64) & (q_row % 64 // 2 == q_col % 32))
+    p_low = group8 % 2 == 0
     message = dot(adjusted, reorder).reshape(NB, 8, 128)
     for b in range(NB):
-        left_g[:, lanes(b)] = jnp.concatenate([message[b], jnp.zeros((8, 128), F32)], axis=0).astype(BF16)
+        left_g[:, lanes(b)] = jnp.concatenate(
+            [jnp.where(p_low, message[b], 0.0), jnp.where(p_low, 0.0, message[b])], axis=0
+        ).astype(BF16)
 
     def second(b, carry):
         r = product(b)
         at_low = group8 < 2
-        p_low = group8 % 2 == 0
-        one, two = jnp.where(at_low, r[0], r[2]), jnp.where(at_low, r[1], r[3])
-        rows = jnp.concatenate(
-            [jnp.where(p_low, one, 0.0), jnp.where(p_low, two, 0.0), jnp.where(p_low, 0.0, one), jnp.where(p_low, 0.0, two)],
-            axis=0,
-        )
+        rows = jnp.concatenate([jnp.where(at_low, r[0], r[2]), jnp.where(at_low, r[1], r[3])], axis=0)
         top = rows.astype(BF16)
         at = pl.ds(pl.multiple_of(128 * b, 128), 128)
         high_g[:, at] = top
@@ -294,55 +283,61 @@
 
     lax.fori_loop(0, NB, second, 0, unroll=8)
     galerkin = (dot_t(left_g[...], high_g[...]) + dot_t(left_g[...], low_g[...])) * (NB * 64) ** -0.5
-    terms[s] = jnp.concatenate([galerkin[0:8], jnp.zeros((8, 96), F32)], axis=1)
-    to_sub(lambda d: terms.at[s], terms, 3)
-
-    settle(terms, S - 1, 7)
-    every = terms[...].reshape(256, 128)
-    top = every.astype(BF16)
-    both = jnp.concatenate([top, (every - top.astype(F32)).astype(BF16)], axis=0)
-    wide = dot(both, copies)
-    wide_row, wide_lane = iota((512, 256), 0), iota((512, 256), 1)
-    wide = jnp.where(wide_row // 8 % 8 == wide_lane // 16 % 8, wide, 0.0).astype(BF16)
-    parts = []
-    for v in range(4):
-        pieces_v = [wide[256 * h + 64 * v : 256 * h + 64 * v + 64, 128 * p : 128 * p + 128] for h in range(2) for p in range(2)]
-        parts.append(dot(rows_mine[:, 256 * v : 256 * v + 256], jnp.concatenate(pieces_v, axis=0)))
-    part = jnp.concatenate(parts, axis=1)
-    p1 = part.astype(BF16).astype(F32)
-    p2 = (part - p1).astype(BF16).astype(F32)
-    p3 = part - p1 - p2
-    out = dot(jnp.concatenate([p1, p2, p3], axis=0).astype(BF16), spread_cols)
-    out = out[0:16] + out[16:32] + out[32:48]
-    for v in range(G):
-        piece[v] = out[4 * (v // 4) : 4 * (v // 4) + 4, 128 * (v % 4) : 128 * (v % 4) + 128]
-    to_group(lambda d: piece.at[d], pieces, 4)
-    pieces[g] = piece[g]
-    settle(pieces, G - 1, 9)
-    total = pieces[0]
-    for v in range(1, G):
-        total = total + pieces[v]
-    final[g] = total
-    to_group(lambda d: final.at[g], final, 5)
-    settle(final, G - 1, 11)
-    for v in range(G):
-        matrix[pl.ds(4 * (v // 4), 4), lanes(v % 4)] = final[v]
+    terms_z[g] = jnp.where(place16, jnp.concatenate([galerkin] * 8, axis=1), 0.0).astype(BF16)
+    to_group(lambda d: terms_z.at[g], terms_z, 5)
+
+    settle(maps_s, S - 1, 9)
+
+    def columns(v, carry):
+        maps = maps_s[v].astype(F32)
+        diagonal = iota((16, 256), 0) == iota((16, 256), 1) % 16
+        key = jnp.sum(jnp.where(diagonal, maps, 0.0), axis=0, keepdims=True).astype(jnp.int32) + COARSE // 2
+        spread_t[:, pl.ds(pl.multiple_of(256 * v, 256), 256)] = hot(iota((COARSE, 256), 0) == key)
+        return carry
+
+    lax.fori_loop(0, S, columns, 0)
+    settle(terms_z, G - 1, 11)
+    merge(terms_z, terms_s)
+    to_sub(lambda d: terms_s.at[s], terms_s, 6, lambda step: step // 8)
+
+    row = iota((16, 256), 0).astype(F32) + (lax.convert_element_type(16 * s, F32) - COARSE // 2)
+
+    def gather_rows(v):
+        maps, values = maps_s[v].astype(F32), terms_s[v].astype(F32)
+        total = jnp.zeros((16, 256), F32)
+        for c in range(16):
+            total = total + jnp.where(maps[c : c + 1] == row, values[c : c + 1], 0.0)
+        top = total.astype(BF16)
+        return jnp.concatenate([top, (total - top.astype(F32)).astype(BF16)], axis=0)
+
+    def add(v, total):
+        picked = jnp.concatenate([gather_rows(4 * v + w) for w in range(4)], axis=1)
+        return total + dot_t(picked, spread_t[:, pl.ds(pl.multiple_of(1024 * v, 1024), 1024)])
+
+    total = jnp.zeros((32, COARSE), F32)
+    for dx in (0, 1, 3, 2):
+        settle(terms_s, 8 if dx else 7, 13 + dx)
+        first_of = 2 * lax.rem(lax.div(s, 8) + 4 - dx, 4)
+        total = add(first_of + 1, add(first_of, total))
+    matrix[...] = total[0:16] + total[16:32]
 
     settle(table, S - 1, 0)
     settle(send, S - 1, 2)
     settle(back, S - 1, 4)
-    settle(terms, S - 1, 6)
-    settle(piece, G - 1, 8)
-    settle(final, G - 1, 10)
+    settle(maps_z, G - 1, 6)
+    settle(maps_s, S - 1, 8)
+    settle(terms_z, G - 1, 10)
+    settle(terms_s, S - 1, 12)
 
 
 def on_device(schur_blocks, block_cols, basis, owners, targets, inverses, coarse_map):
-    vmem = pl.BlockSpec(memory_space=pltpu.VMEM)
+    hbm = pl.BlockSpec(memory_space=pltpu.HBM)
+    shapes = (jax.ShapeDtypeStruct((NB, 1024), F32), jax.ShapeDtypeStruct((16, COARSE), F32))
     corrected, matrix = pl.pallas_call(
         kernel,
-        out_shape=(jax.ShapeDtypeStruct((NB, 1024), F32), jax.ShapeDtypeStruct((16, COARSE), F32)),
-        in_specs=[pl.BlockSpec(memory_space=pltpu.HBM)] * 7,
-        out_specs=(vmem, vmem),
+        out_shape=shapes,
+        in_specs=[hbm] * 7,
+        out_specs=(pl.BlockSpec(memory_space=pltpu.VMEM),) * 2,
         scratch_shapes=[
             pltpu.SMEM((KB, 1, NB), jnp.int32),
             pltpu.VMEM((NB, 1024), BF16),
@@ -364,27 +359,33 @@
             pltpu.VMEM((S, 32, 128), BF16),
             pltpu.VMEM((S, 32, 128), BF16),
             pltpu.VMEM((16, 128 * NB), BF16),
-            pltpu.VMEM((32, 128 * NB), BF16),
-            pltpu.VMEM((32, 128 * NB), BF16),
-            pltpu.VMEM((S, 8, 128), F32),
-            pltpu.VMEM((G, 4, 128), F32),
-            pltpu.VMEM((G, 4, 128), F32),
-            pltpu.VMEM((G, 4, 128), F32),
+            pltpu.VMEM((16, 128 * NB), BF16),
+            pltpu.VMEM((16, 128 * NB), BF16),
+            pltpu.VMEM((G, 16, 128), BF16),
+            pltpu.VMEM((S, 16, 256), BF16),
+            pltpu.VMEM((G, 16, 128), BF16),
+            pltpu.VMEM((S, 16, 256), BF16),
+            pltpu.VMEM((COARSE, 256 * S), BF16),
             pltpu.SemaphoreType.DMA((CHUNKS + 6,)),
-            pltpu.SemaphoreType.DMA((12,)),
+            pltpu.SemaphoreType.DMA((17,)),
         ],
         compiler_params=pltpu.CompilerParams(
-            collective_id=0, has_side_effects=True, vmem_limit_bytes=62 * 1024 * 1024
+            collective_id=0, has_side_effects=True, vmem_limit_bytes=48 * 1024 * 1024
         ),
         name="setup_pass",
     )(
-        jnp.swapaxes(schur_blocks[0, 0], 0, 1),
-        jnp.transpose(block_cols, (0, 3, 1, 2))[0],
-        basis[0, 0],
-        owners[0, :, :, 0],
-        targets[0],
-        inverses[0, 0],
-        coarse_map[0],
+        *[
+            pltpu.with_memory_space_constraint(x, pltpu.HBM)
+            for x in (
+                jnp.swapaxes(schur_blocks[0, 0], 0, 1),
+                jnp.transpose(block_cols, (0, 3, 1, 2))[0],
+                basis[0, 0],
+                owners[0, :, :, 0],
+                targets[0],
+                inverses[0, 0],
+                coarse_map[0],
+            )
+        ]
     )
     return corrected[None, None], matrix
 

time: 59 us -> 52.9 us (0.90)
  Pallas kernels: 55.1 us -> 50.9 us
  local copies, waits for them, and re-layouts: 2.94 us -> 1.27 us
    pallas_call x1, Pallas kernels: 55.1 us -> 50.9 us  [on_device(): pl.pallas_call(kernel, out_shape=shapes, in_specs=[hbm] * 7, out_specs=(p...]
    unnamed x2, local copies, waits for them, and re-layouts: 2.94 us -> 1.27 us
where the time goes in v3:
time: 52.9 us; the launch traced here: 52.8 us
  Pallas kernels  50.9 us (96%)
  local copies, waits for them, and re-layouts  1.27 us (2%)
  between operations  0.64 us (1%)
    pallas_call x1, Pallas kernels, on_device(): pl.pallas_call(kernel, out_shape=shapes, in_specs=[hbm] * 7, out_specs=(p...  50.9 us
    unnamed x2, local copies, waits for them, and re-layouts  1.27 us

profile of v3, /device:TPU:1, one launch (start us, length us, event | category | flops | bytes accessed | tf_op | source)
XLA Modules:
  0.0 52.8 jit_solution(3336019174103230786)
XLA Ops:
  0.6 50.9 %setup_pass.1 = (f32[32,1024]{1,0:T(8,128)S(1)}, f32[16,512]{1,0:T(8,128)S(1)}) custom-call(bf16[14,32,4096]{2,1,0:T(8,128)(2,1)} %bitcast.13, s32[14,1,32]{2,1,0:T(1,128)} %bitcast.16, bf16[32,1024]{1,0:T(8,128)(2,1)} %bitcast.15, s32[1,32]{1,0:T(1,128)} %bitcast.17, s32[1,32]{1,0:T(1,128)} %bitcast.18, f32[32,4096]{1,0:T(8,128)} %bitcast.14, s32[1,16]{1,0:T(1,128)} %bitcast.19), custom_call_target="tpu_custom_call" | custom-call | tf_op jit(solution)/shard_map/setup_pass/pallas_call | solution.py:336
  51.5 0.7 %copy.11 = f32[1,1,32,1024]{3,2,1,0:T(8,128)} copy(f32[1,1,32,1024]{3,2,1,0:T(8,128)S(1)} %bitcast.12) | data formatting | bytes 262144
  52.2 0.6 %copy.12 = f32[16,512]{1,0:T(8,128)} copy(f32[16,512]{1,0:T(8,128)S(1)} %get-tuple-element.9) | data formatting | bytes 65536

commit v4 on v3

--- a/solution.py
+++ b/solution.py
@@ -56,6 +56,7 @@
 
 SUB_STEPS = sorted(range(1, S), key=lambda v: -(ring(v // 8, 4) + ring(v // 2 % 4, 4) + 0.5 * (v % 2)))
 GROUP_STEPS = sorted(range(1, G), key=lambda v: -ring(v, G))
+NEAR = (1, 2, 3, 4, 13, 14, 15)
 
 
 def spread(x):
@@ -81,32 +82,28 @@
 
         lax.fori_loop(1, count, body, 0)
 
-    def to_sub(source_of, into, k, landing=lambda step: 0):
-        def one(step):
+    def to_sub(source_of, into, sent, landed):
+        for step in SUB_STEPS:
             d = sub_peer(s, step)
             pltpu.make_async_remote_copy(
-                src_ref=source_of(d), dst_ref=into.at[s], send_sem=sem.at[2 * k], recv_sem=sem.at[2 * k + 1 + landing(step)],
+                src_ref=source_of(d), dst_ref=into.at[s], send_sem=sem.at[sent], recv_sem=sem.at[landed(step)],
                 device_id={"sub": d}, device_id_type=MESH,
             ).start()
 
-        for step in SUB_STEPS:
-            one(step)
-
-    def to_group(source_of, into, k):
-        def one(step):
-            d = group_peer(g, step)
+    def to_group(source_of, into, sent, landed):
+        for step in GROUP_STEPS:
             pltpu.make_async_remote_copy(
-                src_ref=source_of(d), dst_ref=into.at[g], send_sem=sem.at[2 * k], recv_sem=sem.at[2 * k + 1],
-                device_id={"group": d}, device_id_type=MESH,
+                src_ref=source_of(g), dst_ref=into.at[g], send_sem=sem.at[sent], recv_sem=sem.at[landed(step)],
+                device_id={"group": group_peer(g, step)}, device_id_type=MESH,
             ).start()
-
-        for step in GROUP_STEPS:
-            one(step)
 
     def settle(buffer, count, which):
         part = buffer.at[pl.ds(0, count)]
         pltpu.make_async_copy(part, part, sem.at[which]).wait()
 
+    barrier = pltpu.get_barrier_semaphore()
+    for step in GROUP_STEPS:
+        pl.semaphore_signal(barrier, 1, device_id={"group": group_peer(g, step)}, device_id_type=MESH)
     per = KB // CHUNKS
 
     def load(c):
@@ -120,11 +117,7 @@
     for c in range(CHUNKS):
         load(c).start()
     load_inverse = pltpu.make_async_copy(inverse_hbm, inverse, load_sem.at[CHUNKS + 5])
-    load_inverse.start()
-
-    barrier = pltpu.get_barrier_semaphore()
     each(S, lambda step: pl.semaphore_signal(barrier, 1, device_id={"sub": sub_peer(s, step)}, device_id_type=MESH))
-    each(G, lambda step: pl.semaphore_signal(barrier, 1, device_id={"group": group_peer(g, step)}, device_id_type=MESH))
     for copy in small:
         copy.wait()
 
@@ -170,9 +163,7 @@
             for half in range(2):
                 unpack(k, half)
 
-    pl.semaphore_wait(barrier, S - 1 + G - 1)
-    to_sub(lambda d: table.at[s], table, 0)
-    to_group(lambda d: maps_z.at[g], maps_z, 3)
+    load_inverse.start()
 
     def product(b):
         vectors = jnp.concatenate([vecs[cols[k, 0, b]] for k in range(KB)], axis=1)
@@ -194,7 +185,10 @@
     code = slot_lane // CAP * 32 + iota((1, 256), 1) % 8 * CAP + slot_lane % CAP
     select = hot(iota((1024, 256), 0) == code)
     send[...] = dot(select, rows_f32[...].astype(BF16)).astype(BF16).reshape(S, 32, 128)
-    to_sub(lambda d: send.at[d], arrive, 1)
+    pl.semaphore_wait(barrier, S - 1 + G - 1)
+    to_sub(lambda d: table.at[s], table, 0, lambda step: 1)
+    to_sub(lambda d: send.at[d], arrive, 2, lambda step: 3)
+    to_group(lambda d: maps_z.at[d], maps_z, 6, lambda step: 7)
     arrive[s] = send[s]
 
     tall = hot(iota((256, NB), 0) // 8 == iota((256, NB), 1))
@@ -242,21 +236,16 @@
 
     lax.fori_loop(0, NB, correct, 0, unroll=8)
     back[...] = dot(gather_t, rows_f32[...].astype(BF16)).astype(BF16).reshape(S, 32, 128)
-    to_sub(lambda d: back.at[d], returned, 2)
+    to_sub(lambda d: back.at[d], returned, 4, lambda step: 5)
     returned[s] = back[s]
     for u in range(8):
         corrected[:, lanes(u)] = rows_f32[pl.ds(u, NB, stride=8), :]
 
-    def merge(parts, into):
-        for h in range(2):
-            total = parts[8 * h].astype(F32)
-            for v in range(1, 8):
-                total = total + parts[8 * h + v].astype(F32)
-            into[s, :, lanes(h)] = total.astype(BF16)
-
-    settle(maps_z, G - 1, 7)
-    merge(maps_z, maps_s)
-    to_sub(lambda d: maps_s.at[s], maps_s, 4)
+    def merged(parts, half):
+        total = parts[lax.rem(g + (4 if half else 12), G)].astype(F32)
+        for v in range(1, 8):
+            total = total + parts[lax.rem(g + (4 if half else 12) + v, G)].astype(F32)
+        return total.astype(BF16)
 
     settle(returned, S - 1, 5)
     from_owner = dot(select_t[...], returned[...].reshape(1024, 128))
@@ -284,41 +273,54 @@
     lax.fori_loop(0, NB, second, 0, unroll=8)
     galerkin = (dot_t(left_g[...], high_g[...]) + dot_t(left_g[...], low_g[...])) * (NB * 64) ** -0.5
     terms_z[g] = jnp.where(place16, jnp.concatenate([galerkin] * 8, axis=1), 0.0).astype(BF16)
-    to_group(lambda d: terms_z.at[g], terms_z, 5)
+    to_group(lambda d: terms_z.at[d], terms_z, 10, lambda step: 11 if step in NEAR else 12)
+
+    settle(maps_z, G - 1, 7)
+    for half in range(2):
+        maps_s[s, half] = merged(maps_z, half)
+    to_sub(lambda d: maps_s.at[s], maps_s, 8, lambda step: 9)
+
+    settle(terms_z, 7, 11)
+    terms_s[0, s] = merged(terms_z, 0)
+    to_sub(lambda d: terms_s.at[0, s], terms_s.at[0], 13, lambda step: 14)
+    settle(terms_z, 8, 12)
+    terms_s[1, s] = merged(terms_z, 1)
+    to_sub(lambda d: terms_s.at[1, s], terms_s.at[1], 15, lambda step: 16 + step // 8)
 
     settle(maps_s, S - 1, 9)
 
     def columns(v, carry):
-        maps = maps_s[v].astype(F32)
-        diagonal = iota((16, 256), 0) == iota((16, 256), 1) % 16
-        key = jnp.sum(jnp.where(diagonal, maps, 0.0), axis=0, keepdims=True).astype(jnp.int32) + COARSE // 2
-        spread_t[:, pl.ds(pl.multiple_of(256 * v, 256), 256)] = hot(iota((COARSE, 256), 0) == key)
+        diagonal = iota((16, 128), 0) == iota((16, 128), 1) % 16
+        for half in range(2):
+            maps = maps_s[v, half].astype(F32)
+            key = jnp.sum(jnp.where(diagonal, maps, 0.0), axis=0, keepdims=True).astype(jnp.int32) + COARSE // 2
+            spread_t[:, pl.ds(pl.multiple_of(4096 * half + 128 * v, 128), 128)] = hot(iota((COARSE, 128), 0) == key)
         return carry
 
-    lax.fori_loop(0, S, columns, 0)
-    settle(terms_z, G - 1, 11)
-    merge(terms_z, terms_s)
-    to_sub(lambda d: terms_s.at[s], terms_s, 6, lambda step: step // 8)
-
-    row = iota((16, 256), 0).astype(F32) + (lax.convert_element_type(16 * s, F32) - COARSE // 2)
-
-    def gather_rows(v):
-        maps, values = maps_s[v].astype(F32), terms_s[v].astype(F32)
-        total = jnp.zeros((16, 256), F32)
+    lax.fori_loop(0, S, columns, 0, unroll=2)
+
+    row = iota((16, 128), 0).astype(F32) + (lax.convert_element_type(16 * s, F32) - COARSE // 2)
+
+    def gather_rows(half, v):
+        maps, values = maps_s[v, half].astype(F32), terms_s[half, v].astype(F32)
+        total = jnp.zeros((16, 128), F32)
         for c in range(16):
             total = total + jnp.where(maps[c : c + 1] == row, values[c : c + 1], 0.0)
         top = total.astype(BF16)
         return jnp.concatenate([top, (total - top.astype(F32)).astype(BF16)], axis=0)
 
-    def add(v, total):
-        picked = jnp.concatenate([gather_rows(4 * v + w) for w in range(4)], axis=1)
-        return total + dot_t(picked, spread_t[:, pl.ds(pl.multiple_of(1024 * v, 1024), 1024)])
-
+    def add(half, x, total):
+        picked = jnp.concatenate([gather_rows(half, 8 * x + w) for w in range(8)], axis=1)
+        at = 4096 * half + 1024 * x
+        return total + dot_t(picked, spread_t[:, pl.ds(at if isinstance(at, int) else pl.multiple_of(at, 1024), 1024)])
+
+    settle(terms_s.at[0], S - 1, 14)
     total = jnp.zeros((32, COARSE), F32)
+    for x in range(4):
+        total = add(0, x, total)
     for dx in (0, 1, 3, 2):
-        settle(terms_s, 8 if dx else 7, 13 + dx)
-        first_of = 2 * lax.rem(lax.div(s, 8) + 4 - dx, 4)
-        total = add(first_of + 1, add(first_of, total))
+        settle(terms_s.at[1], 8 if dx else 7, 16 + dx)
+        total = add(1, lax.rem(lax.div(s, 8) + 4 - dx, 4), total)
     matrix[...] = total[0:16] + total[16:32]
 
     settle(table, S - 1, 0)
@@ -327,7 +329,8 @@
     settle(maps_z, G - 1, 6)
     settle(maps_s, S - 1, 8)
     settle(terms_z, G - 1, 10)
-    settle(terms_s, S - 1, 12)
+    settle(terms_s.at[0], S - 1, 13)
+    settle(terms_s.at[1], S - 1, 15)
 
 
 def on_device(schur_blocks, block_cols, basis, owners, targets, inverses, coarse_map):
@@ -362,12 +365,12 @@
             pltpu.VMEM((16, 128 * NB), BF16),
             pltpu.VMEM((16, 128 * NB), BF16),
             pltpu.VMEM((G, 16, 128), BF16),
-            pltpu.VMEM((S, 16, 256), BF16),
+            pltpu.VMEM((S, 2, 16, 128), BF16),
             pltpu.VMEM((G, 16, 128), BF16),
-            pltpu.VMEM((S, 16, 256), BF16),
+            pltpu.VMEM((2, S, 16, 128), BF16),
             pltpu.VMEM((COARSE, 256 * S), BF16),
             pltpu.SemaphoreType.DMA((CHUNKS + 6,)),
-            pltpu.SemaphoreType.DMA((17,)),
+            pltpu.SemaphoreType.DMA((20,)),
         ],
         compiler_params=pltpu.CompilerParams(
             collective_id=0, has_side_effects=True, vmem_limit_bytes=48 * 1024 * 1024

time: 52.9 us -> 50.8 us (0.960)
  Pallas kernels: 50.9 us -> 48.8 us
    pallas_call x1, Pallas kernels: 50.9 us -> 48.8 us  [on_device(): pl.pallas_call(kernel, out_shape=shapes, in_specs=[hbm] * 7, out_specs=(p...]
where the time goes in v4:
time: 50.8 us; the launch traced here: 50.7 us
  Pallas kernels  48.8 us (96%)
  local copies, waits for them, and re-layouts  1.27 us (2%)
  between operations  0.64 us (1%)
    pallas_call x1, Pallas kernels, on_device(): pl.pallas_call(kernel, out_shape=shapes, in_specs=[hbm] * 7, out_specs=(p...  48.8 us
    unnamed x2, local copies, waits for them, and re-layouts  1.27 us

profile of v4, /device:TPU:1, one launch (start us, length us, event | category | flops | bytes accessed | tf_op | source)
XLA Modules:
  0.0 50.7 jit_solution(2778619033465134320)
XLA Ops:
  0.6 48.8 %setup_pass.1 = (f32[32,1024]{1,0:T(8,128)S(1)}, f32[16,512]{1,0:T(8,128)S(1)}) custom-call(bf16[14,32,4096]{2,1,0:T(8,128)(2,1)} %bitcast.13, s32[14,1,32]{2,1,0:T(1,128)} %bitcast.16, bf16[32,1024]{1,0:T(8,128)(2,1)} %bitcast.15, s32[1,32]{1,0:T(1,128)} %bitcast.17, s32[1,32]{1,0:T(1,128)} %bitcast.18, f32[32,4096]{1,0:T(8,128)} %bitcast.14, s32[1,16]{1,0:T(1,128)} %bitcast.19), custom_call_target="tpu_custom_call" | custom-call | tf_op jit(solution)/shard_map/setup_pass/pallas_call | solution.py:339
  49.4 0.7 %copy.11 = f32[1,1,32,1024]{3,2,1,0:T(8,128)} copy(f32[1,1,32,1024]{3,2,1,0:T(8,128)S(1)} %bitcast.12) | data formatting | bytes 262144
  50.1 0.6 %copy.12 = f32[16,512]{1,0:T(8,128)} copy(f32[16,512]{1,0:T(8,128)S(1)} %get-tuple-element.9) | data formatting | bytes 65536
